TPU v7x, 128 devices: a whole 4x4x4 slice. The times are simulated.
128 devices in a mesh: dp: 16 (over y, x), tensor: 8 (over z, core).
Axes of the slice: x: 4, y: 4, z: 4, core: 2. Of those that a mesh axis runs over, the one named last changes fastest.
Arguments:
- old_master: float32 [128, 672, 128], P(('dp', 'tensor')), may hold values from -6 to 6
- old_avg: float32 [128, 672, 128], P(('dp', 'tensor')), may hold values from -1.8 to 1.8
- old_sq: float32 [128, 672, 128], P(('dp', 'tensor')), may hold values from 0.001 to 1
- grad: float32 [128, 672, 128], P(('dp', 'tensor')), may hold values from -6 to 6
- old_table: int32 [128, 3], replicated, may hold values from 0 to 10751, as said below
- new_table: int32 [128, 3], replicated, may hold values from 0 to 5375, as said below
- head_order: int32 [112], replicated, may hold values from 0 to 111, each once
Outputs:
- new_master: float32 [128, 672, 128], P(('dp', 'tensor'))
- new_avg: float32 [128, 672, 128], P(('dp', 'tensor'))
- new_sq: float32 [128, 672, 128], P(('dp', 'tensor'))
- params: bfloat16 [128, 43008], P(None, 'tensor')
Inputs may be any that keep to these rules, and one draw needn't show every extreme that they name: `old_table`: row k belongs to old rank k // 32; the fragments of one old rank follow one another in k without gaps and cover its 10752 units; every length is 1 to 672, in each old rank one length is exactly 672, and the last fragment of each old rank has length 1. `new_table`: row k = d * 8 + n belongs to new rank n; for one new rank the ranges follow one another in d without gaps and cover its 5376 units; range d lies within units d * 336 to (d + 3) * 336 - 1; every length is 1 to 672, in each new rank one length is exactly 672 and that range reaches unit (d + 2) * 336 or beyond, and the last range of each new rank has length 1.
All inputs are finite; a program needn't handle non-finite values.
Results may differ from a plain program's by a relative error of at most 0.0033.
Values may be sent and summed in bfloat16 or wider, within the bound.
No kernel may reach another device: no remote copies, remote signals or barrier semaphores. Data moves between devices by JAX's collectives and lax.ppermute only.
A program may use at most 128 MiB of HBM per device.

v0:
```python
import jax
import jax.numpy as jnp
from jax import lax
from jax.sharding import PartitionSpec as P

OLD_TP = 4
STEPS_DONE = 10
beta_first = 0.9
beta_second = 0.95
learn_rate = 0.1
decay_rate = 0.1
epsilon_add = 1e-08


def shifted(shard, axis, by):
    peers = lax.axis_size(axis)
    pairs = [(i, i + by) for i in range(peers) if 0 <= i + by < peers]
    return lax.ppermute(shard, axis, pairs)


def adam_update(master, moment, square, gradient):
    moment_new = beta_first * moment + (1.0 - beta_first) * gradient
    square_new = beta_second * square + (1.0 - beta_second) * gradient * gradient
    moment_hat = moment_new / (1.0 - beta_first**STEPS_DONE)
    square_hat = square_new / (1.0 - beta_second**STEPS_DONE)
    master_new = master - learn_rate * (
        moment_hat / (jnp.sqrt(square_hat) + epsilon_add) + decay_rate * master
    )
    return (master_new, moment_new, square_new)


def pick_units(source, wanted, begin_at, count_of):
    offset = wanted - begin_at
    inside = (offset >= 0) & (offset < count_of)
    safe_index = jnp.clip(offset, 0, source.shape[0] - 1)
    return jnp.where(inside[..., None], source[safe_index], jnp.zeros((), source.dtype))


def owner_slice(whole, begin_at, count_of, slot_size):
    padded = jnp.concatenate([whole, jnp.zeros((slot_size, whole.shape[1]), whole.dtype)], axis=0)
    window = lax.dynamic_slice_in_dim(padded, begin_at, slot_size, 0)
    inside = jnp.arange(slot_size, dtype=jnp.int32) < count_of
    return jnp.where(inside[:, None], window, jnp.zeros((), whole.dtype))


def on_device(old_master, old_avg, old_sq, grad, old_table, new_table, head_order):
    slot_size = old_master.shape[1]
    head_dim = old_master.shape[2]
    head_count = head_order.shape[0]
    dp_count = lax.axis_size("dp")
    tp_count = lax.axis_size("tensor")
    all_count = dp_count * tp_count
    dp_index = lax.axis_index("dp")
    tp_index = lax.axis_index("tensor")
    dev_index = dp_index * tp_count + tp_index
    unit_dev = slot_size // 2
    heads_old = head_count // OLD_TP
    heads_new = head_count // tp_count
    new_units = 3 * heads_new
    rows_dev = unit_dev // (3 * head_count)
    block_units = rows_dev * 3 * heads_old
    old_states = (old_master[0], old_avg[0], old_sq[0])
    frag_start = old_table[dev_index, 1]
    frag_length = old_table[dev_index, 2]
    within = jnp.arange(block_units, dtype=jnp.int32)
    target = jnp.arange(all_count, dtype=jnp.int32)[:, None] * block_units + within[None, :]
    sending = tuple((pick_units(single, target, frag_start, frag_length) for single in old_states))
    arrived = lax.all_to_all(sending, ("dp", "tensor"), split_axis=0, concat_axis=0, tiled=True)
    canonical = tuple(
        (
            single.reshape(OLD_TP, all_count // OLD_TP, block_units, head_dim).sum(axis=1)
            for single in arrived
        )
    )
    order_table = head_order.reshape(tp_count, heads_new)

    def regroup(single):
        weight = single.reshape(OLD_TP, rows_dev, heads_old, 3, head_dim).transpose(1, 0, 2, 3, 4)
        weight = weight.reshape(rows_dev, head_count, 3, head_dim)
        return weight[:, order_table].transpose(1, 0, 3, 2, 4)

    regrouped = tuple((regroup(single) for single in canonical))
    landed = lax.all_to_all(regrouped, "tensor", split_axis=0, concat_axis=0, tiled=True)
    blocks = tuple((single.reshape(unit_dev, head_dim) for single in landed))
    new_start = new_table[dev_index, 1]
    new_length = new_table[dev_index, 2]
    gradient = grad[0]
    stacked = jnp.stack(blocks, axis=0)
    nearby = [stacked]
    for distance in (1, 2):
        nearby.append(shifted(stacked, "dp", -distance))
    joined = jnp.concatenate(nearby, axis=1)
    local_start = new_start - dp_index * unit_dev
    mine = tuple(
        (owner_slice(joined[which], local_start, new_length, slot_size) for which in range(3))
    )
    master_new, moment_new, square_new = adam_update(mine[0], mine[1], mine[2], gradient)
    inside = (jnp.arange(slot_size, dtype=jnp.int32) < new_length)[:, None]
    master_new = jnp.where(inside, master_new, 0.0)
    moment_new = jnp.where(inside, moment_new, 0.0)
    square_new = jnp.where(inside, square_new, 0.0)
    pieces = lax.all_gather(master_new.astype(jnp.bfloat16), "dp", axis=0, tiled=True)
    starts_all = new_table.reshape(dp_count, tp_count, 3)[:, tp_index, 1]
    flat_place = jnp.arange(dp_count * unit_dev, dtype=jnp.int32)
    owner = jnp.sum((flat_place[:, None] >= starts_all[None, :]).astype(jnp.int32), axis=1) - 1
    source_index = owner * slot_size + flat_place - starts_all[owner]
    params_flat = pieces[source_index]
    params = params_flat.reshape(-1, new_units * head_dim)
    return (master_new[None], moment_new[None], square_new[None], params)


def solution(mesh):
    in_specs = (
        P(("dp", "tensor"), None, None),
        P(("dp", "tensor"), None, None),
        P(("dp", "tensor"), None, None),
        P(("dp", "tensor"), None, None),
        P(),
        P(),
        P(),
    )
    out_specs = (
        P(("dp", "tensor"), None, None),
        P(("dp", "tensor"), None, None),
        P(("dp", "tensor"), None, None),
        P(None, "tensor"),
    )
    return jax.shard_map(
        on_device, mesh=mesh, in_specs=in_specs, out_specs=out_specs, check_vma=False
    )
```

profile of v0, /device:TPU:1, one launch (start us, length us, event | category | flops | bytes accessed | tf_op | source)
XLA Modules:
  0.0 457.7 jit_solution(10279314720494581328)
XLA Ops:
  7.2 0.0 copy-start
  7.2 1.4 constant_dynamic-slice_fusion.18
  8.6 0.7 compare_select_fusion
  9.3 0.1 reshape.188
  9.4 0.0 copy-done
  9.5 20.5 %gather_fusion = f32[10752,128]{1,0:T(8,128)} fusion(f32[672,128]{1,0:T(8,128)S(1)} %bitcast.81, s32[11264]{0:T(1024)S(1)} %pad_clamp_fusion), kind=kCustom, calls=%fused_computation | custom fusion | bytes 11053056 | tf_op jit(solution)/shard_map/gather | solution.py:36
  29.9 6.8 %reshape.187 = f32[128,84,128]{2,1,0:T(8,128)} reshape(f32[10752,128]{1,0:T(8,128)} %gather_fusion) | data formatting | bytes 11010048 | tf_op jit(solution)/shard_map/gather | solution.py:36
  36.7 1.4 fusion.9
  38.1 0.0 copy-done.2
  38.1 20.5 %gather_fusion.2 = f32[10752,128]{1,0:T(8,128)} fusion(f32[672,128]{1,0:T(8,128)S(1)} %bitcast.82, s32[11264]{0:T(1024)S(1)} %pad_clamp_fusion), kind=kCustom, calls=%fused_computation.2 | custom fusion | bytes 11053056 | tf_op jit(solution)/shard_map/gather | solution.py:36
  58.6 6.7 %reshape.205 = f32[128,84,128]{2,1,0:T(8,128)} reshape(f32[10752,128]{1,0:T(8,128)} %gather_fusion.2) | data formatting | bytes 11010048 | tf_op jit(solution)/shard_map/gather | solution.py:36
  65.3 0.0 copy-done.3
  65.3 20.5 %gather_fusion.4 = f32[10752,128]{1,0:T(8,128)} fusion(f32[672,128]{1,0:T(8,128)S(1)} %bitcast.83, s32[11264]{0:T(1024)S(1)} %pad_clamp_fusion), kind=kCustom, calls=%fused_computation.4 | custom fusion | bytes 11053056 | tf_op jit(solution)/shard_map/gather | solution.py:36
  85.8 6.7 %reshape.223 = f32[128,84,128]{2,1,0:T(8,128)} reshape(f32[10752,128]{1,0:T(8,128)} %gather_fusion.4) | data formatting | bytes 11010048 | tf_op jit(solution)/shard_map/gather | solution.py:36
  92.5 10.2 %broadcast_select_fusion.2 = (f32[128,84,128]{2,1,0:T(8,128)}, f32[128,84,128]{2,1,0:T(8,128)S(1)}, f32[128,84,128]{2,1,0:T(8,128)S(1)}) fusion(f32[128,84,128]{2,1,0:T(8,128)} %reshape.187, pred[128,84]{1,0:T(8,128)(4,1)S(1)} %fusion.9, f32[128,84,128]{2,1,0:T(8,128)} %reshape.205, f32[128,84,128]{2,1,0:T(8,128)} %reshape.223), kind=kLoop, calls=%fused_computation.12 | loop fusion | flops 4128768 | bytes 33040896 | tf_op jit(solution)/shard_map/jit(_where)/select_n | solution.py:36
  102.6 81.0 %all_to_all.30 = f32[128,84,128]{2,1,0:T(8,128)} all-to-all(f32[128,84,128]{2,1,0:T(8,128)S(1)} %get-tuple-element.42), channel_id=1, replica_groups=mesh['dp'=16,'tensor'=8] {'dp','tensor'}, dimensions={0} | all-to-all | bytes 11010048 | tf_op jit(solution)/shard_map/all_to_all | solution.py:68
  183.7 74.5 %all_to_all.31 = f32[128,84,128]{2,1,0:T(8,128)} all-to-all(f32[128,84,128]{2,1,0:T(8,128)S(1)} %get-tuple-element.41), channel_id=1, replica_groups=mesh['dp'=16,'tensor'=8] {'dp','tensor'}, dimensions={0} | all-to-all | bytes 11010048 | tf_op jit(solution)/shard_map/all_to_all | solution.py:68
  258.2 5.9 %all-to-all-start = ((f32[128,84,128]{2,1,0:T(8,128)}), f32[128,84,128]{2,1,0:T(8,128)}, u32[]{:S(2)}, u32[]{:S(2)}) async-start(f32[128,84,128]{2,1,0:T(8,128)} %get-tuple-element.40), calls=%async_computation | async-start | bytes 11534336 | tf_op jit(solution)/shard_map/all_to_all | solution.py:68
  264.1 0.0 copy-done.6
  264.1 0.1 reshape.181
  264.2 0.1 reshape.198
  264.3 2.9 bitcast_reduce_fusion
  267.2 0.1 reshape.230
  267.3 0.7 gather_fusion.5
  268.0 0.8 copy.44
  268.9 65.9 %all-to-all-done = f32[128,84,128]{2,1,0:T(8,128)} async-done(((f32[128,84,128]{2,1,0:T(8,128)}), f32[128,84,128]{2,1,0:T(8,128)}, u32[]{:S(2)}, u32[]{:S(2)}) %all-to-all-start) | async-done | bytes 5505056 | tf_op jit(solution)/shard_map/all_to_all | solution.py:68
  334.8 3.8 all-to-all-start.5
  338.5 2.9 bitcast_reduce_fusion.1
  341.4 0.1 reshape.212
  341.5 0.7 gather_fusion.3
  342.3 0.8 copy.42
  343.1 1.1 all-to-all-done.5
  344.2 4.2 all-to-all-start.3
  348.4 0.0 all-gather.2.cloned.1.call-start
  348.4 2.9 bitcast_reduce_fusion.2
  351.3 0.0 copy-start.4
  351.3 0.1 reshape.194
  351.4 0.7 gather_fusion.1
  352.1 0.0 copy-start.5
  352.2 0.2 copy.40
  352.4 1.7 all-to-all-done.3
  354.1 9.0 %all_to_all.32 = f32[8,1,3,14,128]{4,1,3,2,0:T(1,128)S(1)} all-to-all(f32[8,1,3,14,128]{4,1,3,2,0:T(1,128)S(1)} %copy.40), channel_id=1, replica_groups=mesh['dp'=16,'tensor'=8] {'tensor'}, dimensions={0} | all-to-all | bytes 344064 | tf_op jit(solution)/shard_map/all_to_all | solution.py:83
  363.1 1.3 collective-permute-start.1
  364.4 1.3 collective-permute-start
  366.3 0.7 iota_compare_fusion.1
  367.0 11.8 %collective-permute-done.1 = f32[3,336,128]{2,1,0:T(8,128)S(1)} collective-permute-done((f32[3,336,128]{2,1,0:T(8,128)S(1)}, f32[3,336,128]{2,1,0:T(8,128)S(1)}, u32[]{:S(2)}, u32[]{:S(2)}) %collective-permute-start.1) | collective-permute-done | bytes 516128 | tf_op jit(solution)/shard_map/ppermute | solution.py:18
  378.8 0.0 collective-permute-done
  378.8 0.1 pad_maximum_fusion
  378.9 0.1 slice_bitcast_fusion.2
  379.0 1.5 fusion.12
  380.6 0.0 all-gather.2.cloned.1.call-update
  380.6 0.0 copy-done.5
  380.6 0.1 reshape.184
  380.7 0.2 dynamic-slice_reduce_fusion
  380.9 0.8 constant_dynamic-slice_fusion.7
  381.6 0.1 convert_reduce_fusion
  381.8 4.3 fusion.10
  386.1 0.6 compare_reduce_fusion.8
  386.7 5.5 %select_select_fusion = s32[5376]{0:T(1024)S(1)} fusion(pred[5376]{0:T(1024)(128)(4,1)S(1)} %get-tuple-element.12, pred[5376]{0:T(1024)(128)(4,1)S(1)} %get-tuple-element.11, pred[5376]{0:T(1024)(128)(4,1)S(1)} %get-tuple-element.10, pred[5376]{0:T(1024)(128)(4,1)S(1)} %get-tuple-element.9, pred[5376]{0:T(1024)(128)(4,1)S(1)} %get-tuple-element.8, ...), kind=kLoop, calls=%fused_computation.62 | loop fusion | flops 48384 | bytes 91428 | tf_op jit(solution)/shard_map/gather | solution.py:106
  392.2 0.1 fusion.11
  392.3 0.0 copy-start.1
  392.4 45.3 %all-gather.2.cloned.1.call-done = bf16[10752,128]{1,0:T(8,128)(2,1)} async-done(((bf16[672,128]{1,0:T(8,128)(2,1)}), bf16[10752,128]{1,0:T(8,128)(2,1)}) %all-gather.2.cloned.1.call-update) | async-done | bytes 2752528 | tf_op jit(solution)/shard_map/all_gather | solution.py:102
  437.6 10.8 %gather_fusion.6 = bf16[5376,128]{1,0:T(8,128)(2,1)S(1)} fusion(bf16[10752,128]{1,0:T(8,128)(2,1)} %all-gather.2.cloned.1.call-done, s32[6144]{0:T(1024)S(1)} %pad_clamp_fusion.1), kind=kCustom, calls=%fused_computation.6 | custom fusion | bytes 2774016 | tf_op jit(solution)/shard_map/gather | solution.py:107
  448.5 2.4 reshape.185
  (15 shorter events, 0.2 us)
Async XLA Ops:
  7.2 2.3 copy-start
  29.9 8.2 %copy-start.2 = (f32[1,672,128]{2,1,0:T(8,128)S(1)}, f32[1,672,128]{2,1,0:T(8,128)}, u32[]{:S(2)}) copy-start(f32[1,672,128]{2,1,0:T(8,128)} %param.8) | copy-start | bytes 1032196
  58.6 6.7 %copy-start.3 = (f32[1,672,128]{2,1,0:T(8,128)S(1)}, f32[1,672,128]{2,1,0:T(8,128)}, u32[]{:S(2)}) copy-start(f32[1,672,128]{2,1,0:T(8,128)} %param.9) | copy-start | bytes 1032196
  258.2 5.9 %copy-start.6 = (s32[112]{0:T(128)S(1)}, s32[112]{0:T(128)}, u32[]{:S(2)}) copy-start(s32[112]{0:T(128)} %param.13) | copy-start | bytes 1348
  258.2 76.6 %all-to-all-start = ((f32[128,84,128]{2,1,0:T(8,128)}), f32[128,84,128]{2,1,0:T(8,128)}, u32[]{:S(2)}, u32[]{:S(2)}) async-start(f32[128,84,128]{2,1,0:T(8,128)} %get-tuple-element.40), calls=%async_computation | async-start | bytes 11534336 | tf_op jit(solution)/shard_map/all_to_all | solution.py:68
  334.8 9.4 %all-to-all-start.5 = ((f32[8,1,3,14,128]{4,1,3,2,0:T(1,128)}), f32[8,1,3,14,128]{4,1,3,2,0:T(1,128)S(1)}, u32[]{:S(2)}, u32[]{:S(2)}) async-start(f32[8,1,3,14,128]{4,1,3,2,0:T(1,128)} %copy.44), calls=%async_computation.5 | async-start | bytes 344064 | tf_op jit(solution)/shard_map/all_to_all | solution.py:83
  344.2 9.9 %all-to-all-start.3 = ((f32[8,1,3,14,128]{4,1,3,2,0:T(1,128)}), f32[8,1,3,14,128]{4,1,3,2,0:T(1,128)S(1)}, u32[]{:S(2)}, u32[]{:S(2)}) async-start(f32[8,1,3,14,128]{4,1,3,2,0:T(1,128)} %copy.42), calls=%async_computation.3 | async-start | bytes 344064 | tf_op jit(solution)/shard_map/all_to_all | solution.py:83
  348.4 89.2 %all-gather.2.cloned.1.call-start = ((), (), s32[]{:S(2)}) async-start(), calls=%async_computation.6 | async-start | bytes 2924544 | tf_op jit(solution)/shard_map/all_gather | solution.py:102
  351.3 27.7 %copy-start.4 = (f32[1,672,128]{2,1,0:T(8,128)S(1)}, f32[1,672,128]{2,1,0:T(8,128)}, u32[]{:S(2)}) copy-start(f32[1,672,128]{2,1,0:T(8,128)} %param.10) | copy-start | bytes 1032196
  352.1 28.4 %copy-start.5 = (s32[128,3]{0,1:T(4,128)S(1)}, s32[128,3]{0,1:T(4,128)}, u32[]{:S(2)}) copy-start(s32[128,3]{0,1:T(4,128)} %param.12) | copy-start | bytes 4612
  363.1 15.7 %collective-permute-start.1 = (f32[3,336,128]{2,1,0:T(8,128)S(1)}, f32[3,336,128]{2,1,0:T(8,128)S(1)}, u32[]{:S(2)}, u32[]{:S(2)}) collective-permute-start(f32[3,336,128]{2,1,0:T(8,128)S(1)} %pad_maximum_fusion.1), channel_id=1, source_target_pairs={{16,0},{24,8},{32,16},{40,24},{48,32},{56,40},{64,48},{72,56},{80,... | collective-permute-start | bytes 1548296 | tf_op jit(solution)/shard_map/ppermute | solution.py:18
  364.4 14.4 %collective-permute-start = (f32[3,336,128]{2,1,0:T(8,128)S(1)}, f32[3,336,128]{2,1,0:T(8,128)S(1)}, u32[]{:S(2)}, u32[]{:S(2)}) collective-permute-start(f32[3,336,128]{2,1,0:T(8,128)S(1)} %pad_maximum_fusion.1), channel_id=1, source_target_pairs={{8,0},{16,8},{24,16},{32,24},{40,32},{48,40},{56,48},{64,56},{72,6... | collective-permute-start | bytes 1548296 | tf_op jit(solution)/shard_map/ppermute | solution.py:18
  392.3 58.5 %copy-start.1 = (f32[1,672,128]{2,1,0:T(8,128)S(1)}, f32[1,672,128]{2,1,0:T(8,128)}, u32[]{:S(2)}) copy-start(f32[1,672,128]{2,1,0:T(8,128)} %param.7) | copy-start | bytes 1032196
Sparse Core Ops, SparseCore 0:
  380.7 56.8 all-gather.1
where the time goes:
time: 459 us; the launch traced here: 458 us
  blocking collectives  164 us (36%)
  waiting for transfers between devices  126 us (27%)
  local copies, waits for them, and re-layouts  102 us (22%)
  other arithmetic  34 us (7%)
  starting transfers between devices  16.5 us (4%)
  between operations  15 us (3%)
    all_to_all x2, blocking collectives, on_device(): lax.all_to_all(sending, ('dp', 'tensor'), split_axis=0, concat_axis=0, ti...  156 us
    gather x6, local copies, waits for them, and re-layouts, pick_units(): source[safe_index]  81.6 us
    all_to_all x1, waiting for transfers between devices, on_device(): lax.all_to_all(sending, ('dp', 'tensor'), split_axis=0, concat_axis=0, ti...  65.9 us
    all_gather x1, waiting for transfers between devices, on_device(): lax.all_gather(master_new.astype(jnp.bfloat16), 'dp', axis=0, tiled=True)  45.3 us
    ppermute x2, waiting for transfers between devices, shifted(): return lax.ppermute(shard, axis, pairs)  11.8 us
    gather x1, local copies, waits for them, and re-layouts, on_device(): params_flat = pieces[source_index]  10.8 us
    gather x3, other arithmetic, on_device(): source_index = owner * slot_size + flat_place - starts_all[owner]  10.4 us
    select_n x1, other arithmetic, pick_units(): jnp.where(inside[..., None], source[safe_index], jnp.zeros((), source.dty...  10.2 us
  transfers between devices with their start and end apart: 6, of which 5 were waited for; matrix products, arithmetic and copies ran while one was open for 6% of the time, Pallas kernels for 0%

commit v1 on v0

--- a/solution.py
+++ b/solution.py
@@ -99,7 +99,10 @@
     master_new = jnp.where(inside, master_new, 0.0)
     moment_new = jnp.where(inside, moment_new, 0.0)
     square_new = jnp.where(inside, square_new, 0.0)
-    pieces = lax.all_gather(master_new.astype(jnp.bfloat16), "dp", axis=0, tiled=True)
+    local_array = master_new.astype(jnp.bfloat16)
+    pieces = jnp.concatenate(
+        lax.all_to_all(jnp.stack([local_array for _ in range(lax.psum(1, "dp"))]), "dp", 0, 0), 0
+    )
     starts_all = new_table.reshape(dp_count, tp_count, 3)[:, tp_index, 1]
     flat_place = jnp.arange(dp_count * unit_dev, dtype=jnp.int32)
     owner = jnp.sum((flat_place[:, None] >= starts_all[None, :]).astype(jnp.int32), axis=1) - 1

time: 459 us -> 459 us (level)
  starting transfers between devices: 16.5 us -> 34.3 us
  waiting for transfers between devices: 126 us -> 110 us
  between operations: 15 us -> 1.63 us
  other arithmetic: 34 us -> 41.1 us
    all_gather x1 -> x0, waiting for transfers between devices: 45.3 us -> none  [on_device(): lax.all_gather(master_new.astype(jnp.bfloat16), 'dp', axis=0, tiled=True)]
    all_to_all x0 -> x1, waiting for transfers between devices: none -> 29.5 us  [on_device(): lax.all_to_all(jnp.stack([local_array for _ in range(lax.psum(1, 'dp'))])...]
    all_to_all x0 -> x1, starting transfers between devices: none -> 17.8 us  [on_device(): lax.all_to_all(jnp.stack([local_array for _ in range(lax.psum(1, 'dp'))])...]
    slice x0 -> x1, other arithmetic: none -> 6.77 us  [on_device(): joined[which]]
where the time goes in v1:
time: 459 us; the launch traced here: 458 us
  blocking collectives  164 us (36%)
  waiting for transfers between devices  110 us (24%)
  local copies, waits for them, and re-layouts  106 us (23%)
  other arithmetic  41.1 us (9%)
  starting transfers between devices  34.3 us (7%)
    all_to_all x2, blocking collectives, on_device(): lax.all_to_all(sending, ('dp', 'tensor'), split_axis=0, concat_axis=0, ti...  156 us
    gather x6, local copies, waits for them, and re-layouts, pick_units(): source[safe_index]  81.6 us
    all_to_all x1, waiting for transfers between devices, on_device(): lax.all_to_all(sending, ('dp', 'tensor'), split_axis=0, concat_axis=0, ti...  65.9 us
    all_to_all x1, waiting for transfers between devices, on_device(): lax.all_to_all(jnp.stack([local_array for _ in range(lax.psum(1, 'dp'))])...  29.5 us
    all_to_all x1, starting transfers between devices, on_device(): lax.all_to_all(jnp.stack([local_array for _ in range(lax.psum(1, 'dp'))])...  17.8 us
    ppermute x2, waiting for transfers between devices, shifted(): return lax.ppermute(shard, axis, pairs)  11.8 us
    gather x1, local copies, waits for them, and re-layouts, on_device(): params_flat = pieces[source_index]  11.6 us
    gather x3, other arithmetic, on_device(): source_index = owner * slot_size + flat_place - starts_all[owner]  10.4 us
  transfers between devices with their start and end apart: 6, of which 5 were waited for; matrix products, arithmetic and copies ran while one was open for 6% of the time, Pallas kernels for 0%

profile of v1, /device:TPU:1, one launch (start us, length us, event | category | flops | bytes accessed | tf_op | source)
XLA Modules:
  0.0 457.9 jit_solution(2171286147924405691)
XLA Ops:
  0.6 0.0 copy-start
  0.7 1.4 constant_dynamic-slice_fusion.18
  2.0 0.7 compare_select_fusion
  2.8 0.1 reshape.194
  2.9 0.0 copy-done
  2.9 20.5 %gather_fusion = f32[10752,128]{1,0:T(8,128)} fusion(f32[672,128]{1,0:T(8,128)S(1)} %bitcast.77, s32[11264]{0:T(1024)S(1)} %pad_clamp_fusion), kind=kCustom, calls=%fused_computation | custom fusion | bytes 11053056 | tf_op jit(solution)/shard_map/gather | solution.py:36
  23.4 6.8 %reshape.193 = f32[128,84,128]{2,1,0:T(8,128)} reshape(f32[10752,128]{1,0:T(8,128)} %gather_fusion) | data formatting | bytes 11010048 | tf_op jit(solution)/shard_map/gather | solution.py:36
  30.2 1.4 fusion.9
  31.6 0.0 copy-done.2
  31.6 20.5 %gather_fusion.2 = f32[10752,128]{1,0:T(8,128)} fusion(f32[672,128]{1,0:T(8,128)S(1)} %bitcast.78, s32[11264]{0:T(1024)S(1)} %pad_clamp_fusion), kind=kCustom, calls=%fused_computation.2 | custom fusion | bytes 11053056 | tf_op jit(solution)/shard_map/gather | solution.py:36
  52.0 6.7 %reshape.211 = f32[128,84,128]{2,1,0:T(8,128)} reshape(f32[10752,128]{1,0:T(8,128)} %gather_fusion.2) | data formatting | bytes 11010048 | tf_op jit(solution)/shard_map/gather | solution.py:36
  58.8 0.0 copy-done.3
  58.8 20.5 %gather_fusion.4 = f32[10752,128]{1,0:T(8,128)} fusion(f32[672,128]{1,0:T(8,128)S(1)} %bitcast.79, s32[11264]{0:T(1024)S(1)} %pad_clamp_fusion), kind=kCustom, calls=%fused_computation.4 | custom fusion | bytes 11053056 | tf_op jit(solution)/shard_map/gather | solution.py:36
  79.3 6.7 %reshape.229 = f32[128,84,128]{2,1,0:T(8,128)} reshape(f32[10752,128]{1,0:T(8,128)} %gather_fusion.4) | data formatting | bytes 11010048 | tf_op jit(solution)/shard_map/gather | solution.py:36
  85.9 10.2 %broadcast_select_fusion.2 = (f32[128,84,128]{2,1,0:T(8,128)}, f32[128,84,128]{2,1,0:T(8,128)S(1)}, f32[128,84,128]{2,1,0:T(8,128)S(1)}) fusion(f32[128,84,128]{2,1,0:T(8,128)} %reshape.193, pred[128,84]{1,0:T(8,128)(4,1)S(1)} %fusion.9, f32[128,84,128]{2,1,0:T(8,128)} %reshape.211, f32[128,84,128]{2,1,0:T(8,128)} %reshape.229), kind=kLoop, calls=%fused_computation.12 | loop fusion | flops 4128768 | bytes 33040896 | tf_op jit(solution)/shard_map/jit(_where)/select_n | solution.py:36
  96.1 81.0 %all_to_all.35 = f32[128,84,128]{2,1,0:T(8,128)} all-to-all(f32[128,84,128]{2,1,0:T(8,128)S(1)} %get-tuple-element.42), channel_id=1, replica_groups=mesh['dp'=16,'tensor'=8] {'dp','tensor'}, dimensions={0} | all-to-all | bytes 11010048 | tf_op jit(solution)/shard_map/all_to_all | solution.py:68
  177.1 74.5 %all_to_all.36 = f32[128,84,128]{2,1,0:T(8,128)} all-to-all(f32[128,84,128]{2,1,0:T(8,128)S(1)} %get-tuple-element.41), channel_id=1, replica_groups=mesh['dp'=16,'tensor'=8] {'dp','tensor'}, dimensions={0} | all-to-all | bytes 11010048 | tf_op jit(solution)/shard_map/all_to_all | solution.py:68
  251.6 5.9 %all-to-all-start = ((f32[128,84,128]{2,1,0:T(8,128)}), f32[128,84,128]{2,1,0:T(8,128)}, u32[]{:S(2)}, u32[]{:S(2)}) async-start(f32[128,84,128]{2,1,0:T(8,128)} %get-tuple-element.40), calls=%async_computation | async-start | bytes 11534336 | tf_op jit(solution)/shard_map/all_to_all | solution.py:68
  257.5 0.0 copy-done.6
  257.6 0.1 reshape.186
  257.6 0.1 reshape.204
  257.7 2.9 bitcast_reduce_fusion
  260.6 0.1 reshape.236
  260.7 0.7 gather_fusion.5
  261.5 0.8 copy.45
  262.3 65.9 %all-to-all-done = f32[128,84,128]{2,1,0:T(8,128)} async-done(((f32[128,84,128]{2,1,0:T(8,128)}), f32[128,84,128]{2,1,0:T(8,128)}, u32[]{:S(2)}, u32[]{:S(2)}) %all-to-all-start) | async-done | bytes 5505056 | tf_op jit(solution)/shard_map/all_to_all | solution.py:68
  328.2 3.8 all-to-all-start.5
  332.0 2.9 bitcast_reduce_fusion.1
  334.9 0.1 reshape.218
  335.0 0.7 gather_fusion.3
  335.7 0.8 copy.43
  336.6 1.1 all-to-all-done.5
  337.7 4.2 all-to-all-start.3
  341.9 2.9 bitcast_reduce_fusion.2
  344.8 0.0 copy-start.4
  344.8 0.1 reshape.200
  344.9 0.7 gather_fusion.1
  345.6 0.2 copy.41
  345.8 1.7 all-to-all-done.3
  347.5 9.0 %all_to_all.37 = f32[8,1,3,14,128]{4,1,3,2,0:T(1,128)S(1)} all-to-all(f32[8,1,3,14,128]{4,1,3,2,0:T(1,128)S(1)} %copy.41), channel_id=1, replica_groups=mesh['dp'=16,'tensor'=8] {'tensor'}, dimensions={0} | all-to-all | bytes 344064 | tf_op jit(solution)/shard_map/all_to_all | solution.py:83
  356.5 0.4 pad_maximum_fusion
  357.0 1.3 collective-permute-start.1
  358.3 1.3 collective-permute-start
  360.2 0.7 iota_compare_fusion.1
  360.9 11.8 %collective-permute-done.1 = f32[3,336,128]{2,1,0:T(8,128)S(1)} collective-permute-done((f32[3,336,128]{2,1,0:T(8,128)S(1)}, f32[3,336,128]{2,1,0:T(8,128)S(1)}, u32[]{:S(2)}, u32[]{:S(2)}) %collective-permute-start.1) | collective-permute-done | bytes 516128 | tf_op jit(solution)/shard_map/ppermute | solution.py:18
  372.7 0.3 copy.49
  373.0 0.0 collective-permute-done
  373.0 0.3 copy.48
  373.3 6.8 %pad_maximum_fusion.6 = (f32[1,1008,128]{2,0,1:T(1,128)S(1)}, f32[1,1008,128]{2,0,1:T(1,128)S(1)}, f32[1,1008,128]{2,0,1:T(1,128)S(1)}) fusion(f32[3,336,128]{2,0,1:T(4,128)S(1)} %copy.49, f32[3,336,128]{2,0,1:T(4,128)S(1)} %copy.48, f32[1,336,128]{2,0,1:T(1,128)S(1)} %bitcast.85, f32[1,336,128]{2,0,1:T(1,128)S(1)} %bitcast.87, f32[1,336,128]{2,0,1:T(1,128)S(1)} %bitcast.89), kind=kLoop, calls=%fused_computation.22 | loop fusion | flops 1548288 | bytes 3096576 | tf_op jit(solution)/shard_map/slice | solution.py:95
  380.1 0.0 copy-start.5
  380.1 1.5 fusion.12
  381.5 1.9 stack.5
  383.5 17.8 %all-to-all-start.6 = ((bf16[16,672,128]{2,1,0:T(8,128)(2,1)}), bf16[16,672,128]{2,1,0:T(8,128)(2,1)S(1)}, u32[]{:S(2)}, u32[]{:S(2)}) async-start(bf16[16,672,128]{2,1,0:T(8,128)(2,1)} %stack.5), calls=%async_computation.6 | async-start | bytes 5505024 | tf_op jit(solution)/shard_map/all_to_all | solution.py:104
  401.3 0.1 reshape.190
  401.4 0.2 dynamic-slice_reduce_fusion
  401.5 0.7 constant_dynamic-slice_fusion.7
  402.3 0.1 convert_reduce_fusion
  402.5 4.4 fusion.10
  406.8 0.6 compare_reduce_fusion.8
  407.4 5.5 %select_select_fusion = s32[5376]{0:T(1024)S(1)} fusion(pred[5376]{0:T(1024)(128)(4,1)S(1)} %get-tuple-element.12, pred[5376]{0:T(1024)(128)(4,1)S(1)} %get-tuple-element.11, pred[5376]{0:T(1024)(128)(4,1)S(1)} %get-tuple-element.10, pred[5376]{0:T(1024)(128)(4,1)S(1)} %get-tuple-element.9, pred[5376]{0:T(1024)(128)(4,1)S(1)} %get-tuple-element.8, ...), kind=kLoop, calls=%fused_computation.64 | loop fusion | flops 48384 | bytes 91428 | tf_op jit(solution)/shard_map/gather | solution.py:109
  412.9 0.1 fusion.11
  413.0 29.5 %all-to-all-done.6 = bf16[16,672,128]{2,1,0:T(8,128)(2,1)S(1)} async-done(((bf16[16,672,128]{2,1,0:T(8,128)(2,1)}), bf16[16,672,128]{2,1,0:T(8,128)(2,1)S(1)}, u32[]{:S(2)}, u32[]{:S(2)}) %all-to-all-start.6) | async-done | bytes 2752544 | tf_op jit(solution)/shard_map/all_to_all | solution.py:104
  442.6 11.6 %gather_fusion.6 = bf16[5376,128]{1,0:T(8,128)(2,1)} fusion(bf16[10752,128]{1,0:T(8,128)(2,1)S(1)} %bitcast.80, s32[6144]{0:T(1024)S(1)} %pad_clamp_fusion.1), kind=kCustom, calls=%fused_computation.6 | custom fusion | bytes 2774016 | tf_op jit(solution)/shard_map/gather | solution.py:110
  454.2 3.7 reshape.191
  (17 shorter events, 0.2 us)
Async XLA Ops:
  0.6 2.3 copy-start
  23.4 8.2 %copy-start.2 = (f32[1,672,128]{2,1,0:T(8,128)S(1)}, f32[1,672,128]{2,1,0:T(8,128)}, u32[]{:S(2)}) copy-start(f32[1,672,128]{2,1,0:T(8,128)} %param.8) | copy-start | bytes 1032196
  52.0 6.7 %copy-start.3 = (f32[1,672,128]{2,1,0:T(8,128)S(1)}, f32[1,672,128]{2,1,0:T(8,128)}, u32[]{:S(2)}) copy-start(f32[1,672,128]{2,1,0:T(8,128)} %param.9) | copy-start | bytes 1032196
  251.6 5.9 %copy-start.6 = (s32[112]{0:T(128)S(1)}, s32[112]{0:T(128)}, u32[]{:S(2)}) copy-start(s32[112]{0:T(128)} %param.13) | copy-start | bytes 1348
  251.6 76.6 %all-to-all-start = ((f32[128,84,128]{2,1,0:T(8,128)}), f32[128,84,128]{2,1,0:T(8,128)}, u32[]{:S(2)}, u32[]{:S(2)}) async-start(f32[128,84,128]{2,1,0:T(8,128)} %get-tuple-element.40), calls=%async_computation | async-start | bytes 11534336 | tf_op jit(solution)/shard_map/all_to_all | solution.py:68
  328.2 9.4 %all-to-all-start.5 = ((f32[8,1,3,14,128]{4,1,3,2,0:T(1,128)}), f32[8,1,3,14,128]{4,1,3,2,0:T(1,128)S(1)}, u32[]{:S(2)}, u32[]{:S(2)}) async-start(f32[8,1,3,14,128]{4,1,3,2,0:T(1,128)} %copy.45), calls=%async_computation.5 | async-start | bytes 344064 | tf_op jit(solution)/shard_map/all_to_all | solution.py:83
  337.7 9.9 %all-to-all-start.3 = ((f32[8,1,3,14,128]{4,1,3,2,0:T(1,128)}), f32[8,1,3,14,128]{4,1,3,2,0:T(1,128)S(1)}, u32[]{:S(2)}, u32[]{:S(2)}) async-start(f32[8,1,3,14,128]{4,1,3,2,0:T(1,128)} %copy.43), calls=%async_computation.3 | async-start | bytes 344064 | tf_op jit(solution)/shard_map/all_to_all | solution.py:83
  344.8 35.3 %copy-start.4 = (f32[1,672,128]{2,1,0:T(8,128)S(1)}, f32[1,672,128]{2,1,0:T(8,128)}, u32[]{:S(2)}) copy-start(f32[1,672,128]{2,1,0:T(8,128)} %param.10) | copy-start | bytes 1032196
  357.0 15.7 %collective-permute-start.1 = (f32[3,336,128]{2,1,0:T(8,128)S(1)}, f32[3,336,128]{2,1,0:T(8,128)S(1)}, u32[]{:S(2)}, u32[]{:S(2)}) collective-permute-start(f32[3,336,128]{2,1,0:T(8,128)S(1)} %copy.46), channel_id=1, source_target_pairs={{16,0},{24,8},{32,16},{40,24},{48,32},{56,40},{64,48},{72,56},{80,... | collective-permute-start | bytes 1548296 | tf_op jit(solution)/shard_map/ppermute | solution.py:18
  358.3 14.7 %collective-permute-start = (f32[3,336,128]{2,1,0:T(8,128)S(1)}, f32[3,336,128]{2,1,0:T(8,128)S(1)}, u32[]{:S(2)}, u32[]{:S(2)}) collective-permute-start(f32[3,336,128]{2,1,0:T(8,128)S(1)} %copy.46), channel_id=1, source_target_pairs={{8,0},{16,8},{24,16},{32,24},{40,32},{48,40},{56,48},{64,56},{72,6... | collective-permute-start | bytes 1548296 | tf_op jit(solution)/shard_map/ppermute | solution.py:18
  380.1 21.2 %copy-start.5 = (s32[128,3]{0,1:T(4,128)S(1)}, s32[128,3]{0,1:T(4,128)}, u32[]{:S(2)}) copy-start(s32[128,3]{0,1:T(4,128)} %param.12) | copy-start | bytes 4612
  383.5 59.1 %all-to-all-start.6 = ((bf16[16,672,128]{2,1,0:T(8,128)(2,1)}), bf16[16,672,128]{2,1,0:T(8,128)(2,1)S(1)}, u32[]{:S(2)}, u32[]{:S(2)}) async-start(bf16[16,672,128]{2,1,0:T(8,128)(2,1)} %stack.5), calls=%async_computation.6 | async-start | bytes 5505024 | tf_op jit(solution)/shard_map/all_to_all | solution.py:104
  442.6 15.4 %copy-start.1 = (f32[1,672,128]{2,1,0:T(8,128)S(1)}, f32[1,672,128]{2,1,0:T(8,128)}, u32[]{:S(2)}) copy-start(f32[1,672,128]{2,1,0:T(8,128)} %param.7) | copy-start | bytes 1032196
